TPU v7x, 32 devices: a whole 2x2x4 slice. The times are simulated.
32 devices in a mesh: ctx: 8 (over y, x, core), tp: 4 (over z).
Axes of the slice: x: 2, y: 2, z: 4, core: 2. Of those that a mesh axis runs over, the one named last changes fastest.
Arguments:
- query_proj: bfloat16 [1024, 4096], P('ctx', 'tp'), may hold values from -6 to 6
- key_proj: bfloat16 [1024, 4096], P('ctx', 'tp'), may hold values from -6 to 6
- value_proj: bfloat16 [1024, 4096], P('ctx', 'tp'), may hold values from -6 to 6
- cotangent: bfloat16 [1024, 4096], P('ctx', 'tp'), may hold values from -6 to 6
- filter_taps: float32 [1024, 4096], P('ctx', 'tp'), may hold values from -1 to 1
- short_weights: float32 [3, 3, 4096], P(None, None, 'tp'), may hold values from -3.5 to 3.5
Outputs:
- gated_out: bfloat16 [1024, 4096], P('ctx', 'tp')
- query_grad: bfloat16 [1024, 4096], P('ctx', 'tp')
- key_grad: bfloat16 [1024, 4096], P('ctx', 'tp')
- value_grad: bfloat16 [1024, 4096], P('ctx', 'tp')
- filter_grad: float32 [1024, 4096], P('ctx', 'tp')
- short_grad: float32 [3, 3, 4096], P(None, None, 'tp')
All inputs are finite; a program needn't handle non-finite values.
Results may differ from a plain program's by a relative error of at most 0.0065.
Values may be sent and summed in bfloat16 or wider, within the bound.
No kernel may reach another device: no remote copies, remote signals or barrier semaphores. Data moves between devices by JAX's collectives and lax.ppermute only.
A program may use at most 64 MiB of HBM per device.

v0:
```python
import functools
import math

import jax
import jax.numpy as jnp
import numpy as np
from jax import lax
from jax.experimental import pallas as pl
from jax.experimental.pallas import tpu as pltpu
from jax.sharding import PartitionSpec as P

F32 = jnp.float32
BF16 = jnp.bfloat16
LANES = 128
PHASES = 4
TILE = 16
IN_ARRAYS = 5
OUT_ARRAYS = 5
PIECES = 3


def phase_order(tokens, back):
    rows = lax.broadcasted_iota(jnp.int32, (tokens, tokens), 0)
    cols = lax.broadcasted_iota(jnp.int32, (tokens, tokens), 1)
    grouped, plain = (cols, rows) if back else (rows, cols)
    per = tokens // PHASES
    return (plain == (grouped % per) * PHASES + grouped // per).astype(BF16)


def pack_kernel(query, key, value, cot, taps, packed):
    tokens = query.shape[0]
    order = phase_order(tokens, False)
    for at, source in enumerate((query, key, value, cot, taps)):
        moved = jnp.dot(order, source[...].astype(BF16), preferred_element_type=F32).astype(BF16)
        for block in range(packed.shape[0]):
            packed[block, at * tokens : (at + 1) * tokens, :] = moved[
                :, block * LANES : (block + 1) * LANES
            ]


def pack(arrays, peers):
    tokens, width = arrays[0].shape
    steps = 4 if peers % 4 == 0 else 1
    return pl.pallas_call(
        pack_kernel,
        grid=(steps,),
        in_specs=[pl.BlockSpec((tokens, width // steps), lambda i: (0, i))] * IN_ARRAYS,
        out_specs=pl.BlockSpec((peers // steps, IN_ARRAYS * tokens, LANES), lambda i: (i, 0, 0)),
        out_shape=jax.ShapeDtypeStruct((peers, IN_ARRAYS * tokens, LANES), BF16),
        name="pack_inputs",
    )(*arrays)


def unpack_kernel(packed, gated, query_grad, key_grad, value_grad, filter_grad, short_grad):
    tokens = gated.shape[0]
    order = phase_order(tokens, True)
    rows = short_grad.shape[0] * short_grad.shape[1]
    for block in range(packed.shape[0]):
        lanes = slice(block * LANES, (block + 1) * LANES)
        for at, target in enumerate((gated, query_grad, key_grad, value_grad, filter_grad)):
            part = packed[block, at * tokens : (at + 1) * tokens, :]
            target[:, lanes] = jnp.dot(order, part, preferred_element_type=F32).astype(target.dtype)
        sums = packed[block, OUT_ARRAYS * tokens :, :].astype(F32)
        whole = sums[:rows]
        for piece in range(1, PIECES):
            whole = whole + sums[piece * rows : (piece + 1) * rows]
        for row in range(rows):
            which, tap = divmod(row, short_grad.shape[1])
            short_grad[which, tap : tap + 1, lanes] = whole[row : row + 1]


def unpack(packed, tokens, short_shape):
    peers = packed.shape[0]
    width = peers * LANES
    steps = 4 if peers % 4 == 0 else 1
    spread = pl.BlockSpec((tokens, width // steps), lambda i: (0, i))
    return pl.pallas_call(
        unpack_kernel,
        grid=(steps,),
        in_specs=[pl.BlockSpec((peers // steps, packed.shape[1], LANES), lambda i: (i, 0, 0))],
        out_specs=[spread] * OUT_ARRAYS
        + [pl.BlockSpec(short_shape[:2] + (width // steps,), lambda i: (0, 0, i))],
        out_shape=[jax.ShapeDtypeStruct((tokens, width), BF16)] * 4
        + [
            jax.ShapeDtypeStruct((tokens, width), F32),
            jax.ShapeDtypeStruct(short_shape, F32),
        ],
        name="unpack_outputs",
    )(packed)


@functools.lru_cache(maxsize=None)
def dft_tables(seq_len):
    size = seq_len // PHASES
    k = np.arange(size, dtype=np.int64)[:, None]
    m = np.arange(size, dtype=np.int64)[None, :]
    forward = []
    for phase in range(PHASES):
        turns = ((4 * k + 1) * (PHASES * m + phase)) % (4 * seq_len)
        angle = 2.0 * np.pi / (4 * seq_len) * turns
        forward.append(np.concatenate([np.cos(angle), -np.sin(angle)], axis=0))
    forward = np.stack(forward)
    backward = np.swapaxes(forward, 1, 2) / seq_len

    def pieces(table):
        high = table.astype(BF16)
        low = (table - high.astype(np.float64)).astype(BF16)
        return np.stack([high, low], axis=1)

    return pieces(forward), pieces(backward)


def forward_mix(parts):
    (r0, i0), (r1, i1), (r2, i2), (r3, i3) = parts
    ar, ai, br, bi = r0 + r2, i0 + i2, r0 - r2, i0 - i2
    cr, ci, dr, di = r1 + r3, i1 + i3, r1 - r3, i1 - i3
    return ((ar + cr, ai + ci), (br + di, bi - dr), (ar - cr, ai - ci), (br - di, bi + dr))


def inverse_mix(parts):
    (r0, i0), (r1, i1), (r2, i2), (r3, i3) = parts
    ar, ai, br, bi = r0 + r2, i0 + i2, r0 - r2, i0 - i2
    cr, ci, dr, di = r1 + r3, i1 + i3, r1 - r3, i1 - i3
    return ((ar + cr, ai + ci), (br - di, bi + dr), (ar - cr, ai - ci), (br + di, bi - dr))


def times(left, right):
    return tuple(
        (lr * rr - li * ri, lr * ri + li * rr) for (lr, li), (rr, ri) in zip(left, right)
    )


def conj_times(left, right):
    return tuple(
        (lr * rr + li * ri, lr * ri - li * rr) for (lr, li), (rr, ri) in zip(left, right)
    )


def earlier(phases, by):
    moved = []
    for r in range(PHASES):
        if r >= by:
            moved.append(phases[r - by])
        else:
            last = phases[r - by + PHASES]
            moved.append(jnp.concatenate([jnp.zeros_like(last[:1]), last[:-1]], axis=0))
    return moved


def later(phases, by):
    moved = []
    for r in range(PHASES):
        if r + by < PHASES:
            moved.append(phases[r + by])
        else:
            first = phases[r + by - PHASES]
            moved.append(jnp.concatenate([first[1:], jnp.zeros_like(first[:1])], axis=0))
    return moved


def channel_kernel(
    tokens,
    grad_scale,
    packed,
    weights,
    forward,
    backward,
    out,
    signals,
    spectra,
    high,
    low,
    shorts,
):
    peers = packed.shape[0]
    taps = weights.shape[1]
    size = peers * tokens // PHASES
    per = tokens // PHASES
    at_lanes = pl.ds(pl.multiple_of(lax.axis_index("ctx") * LANES, LANES), LANES)

    def phase_of(array, r):
        start = array * tokens + r * per
        return packed[:, start : start + per, :].reshape(size, LANES)

    def weight(array, tap):
        return weights[array, tap : tap + 1, at_lanes]

    for array in range(3):
        phases = [phase_of(array, r).astype(F32) for r in range(PHASES)]
        summed = [weight(array, 0) * x for x in phases]
        for tap in range(1, taps):
            moved = earlier(phases, tap)
            summed = [s + weight(array, tap) * x for s, x in zip(summed, moved)]
        for r in range(PHASES):
            shorts[array, r] = summed[r]
    for r in range(PHASES):
        signals[r, :, :LANES] = (shorts[1, r] * shorts[2, r]).astype(BF16)
        signals[r, :, LANES : 2 * LANES] = (phase_of(3, r).astype(F32) * shorts[0, r]).astype(BF16)
        signals[r, :, 2 * LANES :] = phase_of(4, r)
        spectra[r] = jnp.dot(
            forward[r, 0], signals[r], preferred_element_type=F32
        ) + jnp.dot(forward[r, 1], signals[r], preferred_element_type=F32)

    for chunk in range(size // TILE):
        real = slice(chunk * TILE, (chunk + 1) * TILE)
        imag = slice(size + chunk * TILE, size + (chunk + 1) * TILE)

        def spectrum(signal):
            lanes = slice(signal * LANES, (signal + 1) * LANES)
            return forward_mix([(spectra[r, real, lanes], spectra[r, imag, lanes]) for r in range(PHASES)])

        prod, grad, filt = spectrum(0), spectrum(1), spectrum(2)
        for which, mixed in enumerate(
            (times(prod, filt), conj_times(filt, grad), conj_times(prod, grad))
        ):
            lanes = slice(which * LANES, (which + 1) * LANES)
            for r, pair in enumerate(inverse_mix(mixed)):
                for rows, part in zip((real, imag), pair):
                    rounded = part.astype(BF16)
                    high[r, rows, lanes] = rounded
                    low[r, rows, lanes] = (part - rounded.astype(F32)).astype(BF16)

    conv, conv_grad = [], []
    for r in range(PHASES):
        result = (
            jnp.dot(backward[r, 0], high[r], preferred_element_type=F32)
            + jnp.dot(backward[r, 0], low[r], preferred_element_type=F32)
            + jnp.dot(backward[r, 1], high[r], preferred_element_type=F32)
        )
        conv.append(result[:, :LANES].astype(BF16).astype(F32))
        conv_grad.append(result[:, LANES : 2 * LANES].astype(BF16).astype(F32))
        out[:, 4 * tokens + r * per : 4 * tokens + (r + 1) * per, :] = (
            (result[:, 2 * LANES :] * grad_scale).astype(BF16).reshape(peers, per, LANES)
        )

    def put(array, r, value):
        start = array * tokens + r * per
        out[:, start : start + per, :] = value.astype(BF16).reshape(peers, per, LANES)

    sums = []
    for array in range(3):
        if array == 0:
            pre = [phase_of(3, r).astype(F32) * conv[r] for r in range(PHASES)]
            for r in range(PHASES):
                put(0, r, shorts[0, r] * conv[r])
        else:
            pre = [conv_grad[r] * shorts[3 - array, r] for r in range(PHASES)]
        total = [weight(array, 0) * x for x in pre]
        for tap in range(1, taps):
            moved = later(pre, tap)
            total = [s + weight(array, tap) * x for s, x in zip(total, moved)]
        for r in range(PHASES):
            put(1 + array, r, total[r])
        phases = [phase_of(array, r).astype(F32) for r in range(PHASES)]
        for tap in range(taps):
            moved = phases if tap == 0 else earlier(phases, tap)
            summed = pre[0] * moved[0]
            for r in range(1, PHASES):
                summed = summed + pre[r] * moved[r]
            sums.append(jnp.sum(summed, axis=0, keepdims=True))
    rest = jnp.concatenate(sums, axis=0) * grad_scale
    pieces = []
    for _ in range(PIECES):
        piece = rest.astype(BF16).astype(F32)
        pieces.append(piece)
        rest = rest - piece
    space = out.shape[1] - OUT_ARRAYS * tokens
    filled = PIECES * len(sums)
    if space > filled:
        pieces.append(jnp.zeros((space - filled, LANES), F32))
    block = jnp.concatenate(pieces, axis=0).astype(BF16)
    for peer in range(peers):
        out[peer, OUT_ARRAYS * tokens :, :] = block


def channel_step(packed, short_weights, tokens):
    peers = packed.shape[0]
    seq_len = peers * tokens
    size = seq_len // PHASES
    forward, backward = dft_tables(seq_len)
    count = PIECES * short_weights.shape[0] * short_weights.shape[1]
    rows = OUT_ARRAYS * tokens + -(-count // TILE) * TILE
    return pl.pallas_call(
        functools.partial(channel_kernel, tokens, 1.0 / math.sqrt(seq_len)),
        in_specs=[pl.BlockSpec(memory_space=pltpu.VMEM)] * 4,
        out_specs=pl.BlockSpec(memory_space=pltpu.VMEM),
        out_shape=jax.ShapeDtypeStruct((peers, rows, LANES), BF16),
        scratch_shapes=[
            pltpu.VMEM((PHASES, size, 3 * LANES), BF16),
            pltpu.VMEM((PHASES, 2 * size, 3 * LANES), F32),
            pltpu.VMEM((PHASES, 2 * size, 3 * LANES), BF16),
            pltpu.VMEM((PHASES, 2 * size, 3 * LANES), BF16),
            pltpu.VMEM((3, PHASES, size, LANES), F32),
        ],
        compiler_params=pltpu.CompilerParams(vmem_limit_bytes=40 * 1024 * 1024),
        name="channel_operator",
    )(packed, short_weights, jnp.asarray(forward), jnp.asarray(backward))


def channel_shards(query_proj, key_proj, value_proj, cotangent, filter_taps, short_weights):
    peers = lax.axis_size("ctx")
    tokens = query_proj.shape[0]
    packed = pack((query_proj, key_proj, value_proj, cotangent, filter_taps), peers)
    packed = lax.all_to_all(packed, "ctx", split_axis=0, concat_axis=0, tiled=True)
    result = channel_step(packed, short_weights, tokens)
    result = lax.all_to_all(result, "ctx", split_axis=0, concat_axis=0, tiled=True)
    return tuple(unpack(result, tokens, short_weights.shape))


def from_behind(array, axis, by):
    peers = lax.axis_size(axis)
    pairs = [(i, i + by) for i in range(peers) if 0 <= i + by < peers]
    return lax.ppermute(array, axis, pairs)


def contract(form, left, right):
    return jnp.einsum(
        form, left, right, precision=lax.Precision.HIGHEST, preferred_element_type=jnp.float32
    )


def table_pair(rows, cols, period):
    row_ids = lax.broadcasted_iota(jnp.int32, (rows, cols), 0)
    col_ids = lax.broadcasted_iota(jnp.int32, (rows, cols), 1)
    angle = 2.0 * math.pi / period * (row_ids * col_ids % period).astype(jnp.float32)
    return (jnp.cos(angle), jnp.sin(angle))


def make_plan(seq_len):
    small_len = int(math.isqrt(2 * seq_len))
    while seq_len % small_len:
        small_len -= 1
    large_len = 2 * seq_len // small_len
    large_cos, large_sin = table_pair(large_len // 2, large_len, large_len)
    small_cos, small_sin = table_pair(small_len, small_len, small_len)
    twist_cos, twist_sin = table_pair(large_len, small_len, small_len * large_len)
    fwd_large = jnp.stack([large_cos, -large_sin], axis=1)
    fwd_small = jnp.stack([jnp.stack([small_cos, -small_sin]), jnp.stack([small_sin, small_cos])])
    inv_small = jnp.stack([jnp.stack([small_cos, small_sin]), jnp.stack([-small_sin, small_cos])])
    inv_large = jnp.stack([large_cos, -large_sin])
    return (small_len, large_len, fwd_large, fwd_small, inv_small, inv_large, twist_cos, twist_sin)


def forward_spec(signal, dft_plan):
    small_len, large_len, fwd_large, fwd_small, inv_small, inv_large, twist_cos, twist_sin = (
        dft_plan
    )
    cube = signal.reshape(signal.shape[0], large_len // 2, small_len)
    section_one = contract("cba,bpk->cpka", cube, fwd_large)
    real_one = section_one[:, 0]
    imag_one = section_one[:, 1]
    section_two = jnp.stack(
        [real_one * twist_cos + imag_one * twist_sin, imag_one * twist_cos - real_one * twist_sin],
        axis=1,
    )
    return contract("cpka,pqaj->cqkj", section_two, fwd_small)


def inverse_half(spec, dft_plan):
    small_len, large_len, fwd_large, fwd_small, inv_small, inv_large, twist_cos, twist_sin = (
        dft_plan
    )
    section_one = contract("cqkj,qpja->cpka", spec, inv_small)
    real_one = section_one[:, 0]
    imag_one = section_one[:, 1]
    section_two = jnp.stack(
        [real_one * twist_cos - imag_one * twist_sin, imag_one * twist_cos + real_one * twist_sin],
        axis=1,
    )
    signal = contract("cpka,pbk->cba", section_two, inv_large)
    return signal.reshape(signal.shape[0], -1) / float(small_len * large_len)


def complex_mul(left, right):
    left_real, left_imag = (left[:, 0], left[:, 1])
    right_real, right_imag = (right[:, 0], right[:, 1])
    return jnp.stack(
        [
            left_real * right_real - left_imag * right_imag,
            left_real * right_imag + left_imag * right_real,
        ],
        axis=1,
    )


def conj_mul(left, right):
    left_real, left_imag = (left[:, 0], left[:, 1])
    right_real, right_imag = (right[:, 0], right[:, 1])
    return jnp.stack(
        [
            left_real * right_real + left_imag * right_imag,
            left_real * right_imag - left_imag * right_real,
        ],
        axis=1,
    )


def conv_forward(prod_chan, filter_spec, dft_plan):
    prod_spec = forward_spec(prod_chan.astype(jnp.float32), dft_plan)
    conv_chan = inverse_half(complex_mul(prod_spec, filter_spec), dft_plan).astype(jnp.bfloat16)
    return (conv_chan, prod_spec)


def conv_backward(grad_chan, filter_spec, prod_spec, dft_plan, grad_scale):
    grad_spec = forward_spec(grad_chan.astype(jnp.float32), dft_plan)
    dconv_chan = inverse_half(conj_mul(filter_spec, grad_spec), dft_plan).astype(jnp.bfloat16)
    dfilter_chan = inverse_half(conj_mul(prod_spec, grad_spec), dft_plan) * grad_scale
    return (dconv_chan, dfilter_chan)


def receive_filter(filter_taps, dft_plan):
    filter_chan = lax.all_to_all(filter_taps.T, "ctx", split_axis=0, concat_axis=1, tiled=True)
    return forward_spec(filter_chan, dft_plan)


def return_filter(dfilter_chan):
    return (
        lax.all_to_all(
            dfilter_chan.astype(jnp.bfloat16), "ctx", split_axis=1, concat_axis=0, tiled=True
        )
        .astype(dfilter_chan.dtype)
        .T
    )


def causal_taps(extended, weights, length, axis):
    rim_rows = len(weights) - 1
    summed = weights[0] * lax.slice_in_dim(extended, rim_rows, rim_rows + length, axis=axis)
    for offset in range(1, len(weights)):
        summed = summed + weights[offset] * lax.slice_in_dim(
            extended, rim_rows - offset, rim_rows - offset + length, axis=axis
        )
    return summed


def reverse_taps(extended, weights, length, axis):
    summed = weights[0] * lax.slice_in_dim(extended, 0, length, axis=axis)
    for offset in range(1, len(weights)):
        summed = summed + weights[offset] * lax.slice_in_dim(
            extended, offset, offset + length, axis=axis
        )
    return summed


def tap_grads(grad_in, extended, tap_count, length, axis):
    rim_rows = tap_count - 1
    rows = [
        jnp.sum(
            grad_in
            * lax.slice_in_dim(extended, rim_rows - offset, rim_rows - offset + length, axis=axis),
            axis=axis,
        )
        for offset in range(tap_count)
    ]
    return jnp.stack(rows, axis=1)


def spread_shards(query_proj, key_proj, value_proj, cotangent, filter_taps, short_weights):
    tokens = query_proj.shape[0]
    tap_count = short_weights.shape[1]
    rim_rows = tap_count - 1
    seq_len = tokens * lax.axis_size("ctx")
    grad_scale = 1.0 / math.sqrt(seq_len)
    dft_plan = make_plan(seq_len)
    stacked = jnp.stack([query_proj, key_proj, value_proj])
    prev_rim = from_behind(stacked[:, tokens - rim_rows :], "ctx", 1)
    extended = jnp.concatenate([prev_rim, stacked], axis=1).astype(jnp.float32)
    weights = [short_weights[:, offset, None, :] for offset in range(tap_count)]
    short_out = causal_taps(extended, weights, tokens, 1)
    product = (short_out[1] * short_out[2]).astype(jnp.bfloat16)
    cot_wide = cotangent.astype(jnp.float32)
    gate_grad = (cot_wide * short_out[0]).astype(jnp.bfloat16)
    filter_spec = receive_filter(filter_taps, dft_plan)
    prod_chan = lax.all_to_all(product.T, "ctx", split_axis=0, concat_axis=1, tiled=True)
    conv_chan, prod_spec = conv_forward(prod_chan, filter_spec, dft_plan)
    conv_tok = lax.all_to_all(conv_chan, "ctx", split_axis=1, concat_axis=0, tiled=True)
    grad_chan = lax.all_to_all(gate_grad.T, "ctx", split_axis=0, concat_axis=1, tiled=True)
    dconv_chan, dfilter_chan = conv_backward(
        grad_chan, filter_spec, prod_spec, dft_plan, grad_scale
    )
    dconv_tok = lax.all_to_all(dconv_chan, "ctx", split_axis=1, concat_axis=0, tiled=True)
    filter_grad = return_filter(dfilter_chan)
    conv_wide = conv_tok.T.astype(jnp.float32)
    dconv_wide = dconv_tok.T.astype(jnp.float32)
    gated = (short_out[0] * conv_wide).astype(jnp.bfloat16)
    token_grads = jnp.stack(
        [cot_wide * conv_wide, dconv_wide * short_out[2], dconv_wide * short_out[1]]
    )
    next_rim = from_behind(token_grads[:, :rim_rows], "ctx", -1)
    grad_ext = jnp.concatenate([token_grads, next_rim], axis=1)
    inputs_grad = reverse_taps(grad_ext, weights, tokens, 1).astype(jnp.bfloat16)
    weight_part = tap_grads(token_grads, extended, tap_count, tokens, 1)
    short_grad = lax.psum(weight_part, "ctx") * grad_scale
    results = (gated, inputs_grad[0], inputs_grad[1], inputs_grad[2])
    return (results[0], results[1], results[2], results[3], filter_grad, short_grad)


def fits(query_proj, filter_taps):
    peers = lax.axis_size("ctx")
    tokens, width = query_proj.shape
    return (
        width == peers * LANES
        and tokens % (PHASES * TILE) == 0
        and peers * tokens <= 2048
    )


def shards(*arrays):
    return channel_shards(*arrays) if fits(arrays[0], arrays[4]) else spread_shards(*arrays)


def solution(mesh):
    placed = (
        P("ctx", "tp"),
        P("ctx", "tp"),
        P("ctx", "tp"),
        P("ctx", "tp"),
        P("ctx", "tp"),
        P(None, None, "tp"),
    )
    return jax.shard_map(
        shards,
        mesh=mesh,
        in_specs=placed,
        out_specs=(
            P("ctx", "tp"),
            P("ctx", "tp"),
            P("ctx", "tp"),
            P("ctx", "tp"),
            P("ctx", "tp"),
            P(None, None, "tp"),
        ),
        check_vma=False,
    )
```

profile of v0, /device:TPU:0, one launch (start us, length us, event | category | flops | bytes accessed | tf_op | source)
XLA Modules:
  0.0 59.3 jit_solution(4792857899038283631)
XLA Ops:
  0.6 0.0 copy-start.1
  0.6 4.2 %pack_inputs.1 = bf16[8,640,128]{2,1,0:T(8,128)(2,1)} custom-call(bf16[128,1024]{1,0:T(8,128)(2,1)} %query.1, bf16[128,1024]{1,0:T(8,128)(2,1)} %key.1, bf16[128,1024]{1,0:T(8,128)(2,1)} %value.1, bf16[128,1024]{1,0:T(8,128)(2,1)} %cot.1, f32[128,1024]{1,0:T(8,128)} %taps.1), custom_call_target="tpu_custom_call" | custom-call | tf_op jit(solution)/shard_map/pack_inputs/pallas_call | solution.py:44
  4.8 0.0 copy-start
  4.8 0.0 copy-start.2
  4.8 23.5 %all_to_all.10.packed = bf16[8,640,128]{2,1,0:T(8,128)(2,1)S(1)} all-to-all(bf16[8,640,128]{2,1,0:T(8,128)(2,1)} %pack_inputs.1), channel_id=1, replica_groups=mesh['ctx'=8,'tp'=4] {'ctx'}, dimensions={0} | all-to-all | bytes 2621440 | tf_op jit(solution)/shard_map/all_to_all | solution.py:304
  28.3 0.0 copy-done.1
  28.3 0.0 copy-done
  28.3 0.0 copy-done.2
  28.3 5.1 %channel_operator.1 = bf16[8,672,128]{2,1,0:T(8,128)(2,1)S(1)} custom-call(bf16[8,640,128]{2,1,0:T(8,128)(2,1)S(1)} %all_to_all.10.packed, f32[3,3,1024]{2,1,0:T(4,128)S(1)} %copy-done.2, bf16[4,2,512,256]{3,2,1,0:T(8,128)(2,1)S(1)} %copy-done.1, bf16[4,2,256,512]{3,2,1,0:T(8,128)(2,1)S(1)} %copy-done), custom_call_target="tpu_custom_call" | custom-call | tf_op jit(solution)/shard_map/channel_operator/pallas_call | solution.py:283
  33.4 22.0 %all_to_all.11.packed = bf16[8,672,128]{2,1,0:T(8,128)(2,1)} all-to-all(bf16[8,672,128]{2,1,0:T(8,128)(2,1)S(1)} %channel_operator.1), channel_id=1, replica_groups=mesh['ctx'=8,'tp'=4] {'ctx'}, dimensions={0} | all-to-all | bytes 2752512 | tf_op jit(solution)/shard_map/all_to_all | solution.py:306
  55.4 3.9 %unpack_outputs.1 = (bf16[128,1024]{1,0:T(8,128)(2,1)}, bf16[128,1024]{1,0:T(8,128)(2,1)}, bf16[128,1024]{1,0:T(8,128)(2,1)}, bf16[128,1024]{1,0:T(8,128)(2,1)},...) custom-call(bf16[8,672,128]{2,1,0:T(8,128)(2,1)} %all_to_all.11.packed), custom_call_target="tpu_custom_call" | custom-call | tf_op jit(solution)/shard_map/unpack_outputs/pallas_call | solution.py:77
Async XLA Ops:
  0.6 27.7 %copy-start.1 = (bf16[4,2,512,256]{3,2,1,0:T(8,128)(2,1)S(1)}, bf16[4,2,512,256]{3,2,1,0:T(8,128)(2,1)}, u32[]{:S(2)}) copy-start(bf16[4,2,512,256]{3,2,1,0:T(8,128)(2,1)} %constant.4.clone.forward) | copy-start | bytes 6291460
  4.8 23.5 %copy-start = (bf16[4,2,256,512]{3,2,1,0:T(8,128)(2,1)S(1)}, bf16[4,2,256,512]{3,2,1,0:T(8,128)(2,1)}, u32[]{:S(2)}) copy-start(bf16[4,2,256,512]{3,2,1,0:T(8,128)(2,1)} %constant.5.clone.backward) | copy-start | bytes 6291460
  4.8 23.5 %copy-start.2 = (f32[3,3,1024]{2,1,0:T(4,128)S(1)}, f32[3,3,1024]{2,1,0:T(4,128)}, u32[]{:S(2)}) copy-start(f32[3,3,1024]{2,1,0:T(4,128)} %weights.1) | copy-start | bytes 110596
where the time goes:
time: 59.6 us; the launch traced here: 59.3 us
  blocking collectives  45.5 us (76%)
  Pallas kernels  13.1 us (22%)
  between operations  0.65 us (1%)
    all_to_all x1, blocking collectives, channel_shards(): lax.all_to_all(packed, 'ctx', split_axis=0, concat_axis=0, tiled=True)  23.5 us
    all_to_all x1, blocking collectives, channel_shards(): lax.all_to_all(result, 'ctx', split_axis=0, concat_axis=0, tiled=True)  22 us
    pallas_call x1, Pallas kernels, channel_step(): pl.pallas_call(functools.partial(channel_kernel, tokens, 1.0 / math.sqrt(...  5.06 us
    pallas_call x1, Pallas kernels, pack(): pl.pallas_call(pack_kernel, grid=(steps,), in_specs=[pl.BlockSpec((tokens...  4.18 us
    pallas_call x1, Pallas kernels, unpack(): pl.pallas_call(unpack_kernel, grid=(steps,), in_specs=[pl.BlockSpec((peer...  3.87 us

commit v1 on v0

--- a/solution.py
+++ b/solution.py
@@ -27,40 +27,55 @@
     return (plain == (grouped % per) * PHASES + grouped // per).astype(BF16)
 
 
-def pack_kernel(query, key, value, cot, taps, packed):
+def partners(peers):
+    return [0] + list(range(peers - 1, 0, -1))
+
+
+def pack_kernel(query, key, value, cot, taps, *packed):
     tokens = query.shape[0]
     order = phase_order(tokens, False)
+    me = lax.axis_index("ctx")
     for at, source in enumerate((query, key, value, cot, taps)):
-        moved = jnp.dot(order, source[...].astype(BF16), preferred_element_type=F32).astype(BF16)
-        for block in range(packed.shape[0]):
-            packed[block, at * tokens : (at + 1) * tokens, :] = moved[
-                :, block * LANES : (block + 1) * LANES
-            ]
+        for step, target in zip(partners(len(packed)), packed):
+            lanes = pl.ds(pl.multiple_of((me ^ step) * LANES, LANES), LANES)
+            moved = jnp.dot(order, source[:, lanes].astype(BF16), preferred_element_type=F32)
+            target[at * tokens : (at + 1) * tokens, :] = moved.astype(BF16)
 
 
 def pack(arrays, peers):
-    tokens, width = arrays[0].shape
-    steps = 4 if peers % 4 == 0 else 1
+    tokens = arrays[0].shape[0]
     return pl.pallas_call(
         pack_kernel,
-        grid=(steps,),
-        in_specs=[pl.BlockSpec((tokens, width // steps), lambda i: (0, i))] * IN_ARRAYS,
-        out_specs=pl.BlockSpec((peers // steps, IN_ARRAYS * tokens, LANES), lambda i: (i, 0, 0)),
-        out_shape=jax.ShapeDtypeStruct((peers, IN_ARRAYS * tokens, LANES), BF16),
+        in_specs=[pl.BlockSpec(memory_space=pltpu.VMEM)] * IN_ARRAYS,
+        out_specs=[pl.BlockSpec(memory_space=pltpu.VMEM)] * peers,
+        out_shape=[jax.ShapeDtypeStruct((IN_ARRAYS * tokens, LANES), BF16)] * peers,
         name="pack_inputs",
     )(*arrays)
 
 
-def unpack_kernel(packed, gated, query_grad, key_grad, value_grad, filter_grad, short_grad):
+def exchange(blocks):
+    peers = len(blocks)
+    got = [blocks[0]]
+    for step, block in list(zip(partners(peers), blocks))[1:]:
+        got.append(lax.ppermute(block, "ctx", [(i, i ^ step) for i in range(peers)]))
+    return got
+
+
+def unpack_kernel(peers, *refs):
+    packed, (gated, query_grad, key_grad, value_grad, filter_grad, short_grad) = (
+        refs[:peers],
+        refs[peers:],
+    )
     tokens = gated.shape[0]
     order = phase_order(tokens, True)
     rows = short_grad.shape[0] * short_grad.shape[1]
-    for block in range(packed.shape[0]):
-        lanes = slice(block * LANES, (block + 1) * LANES)
+    me = lax.axis_index("ctx")
+    for step, source in zip(partners(len(packed)), packed):
+        lanes = pl.ds(pl.multiple_of((me ^ step) * LANES, LANES), LANES)
         for at, target in enumerate((gated, query_grad, key_grad, value_grad, filter_grad)):
-            part = packed[block, at * tokens : (at + 1) * tokens, :]
+            part = source[at * tokens : (at + 1) * tokens, :]
             target[:, lanes] = jnp.dot(order, part, preferred_element_type=F32).astype(target.dtype)
-        sums = packed[block, OUT_ARRAYS * tokens :, :].astype(F32)
+        sums = source[OUT_ARRAYS * tokens :, :].astype(F32)
         whole = sums[:rows]
         for piece in range(1, PIECES):
             whole = whole + sums[piece * rows : (piece + 1) * rows]
@@ -70,23 +85,19 @@
 
 
 def unpack(packed, tokens, short_shape):
-    peers = packed.shape[0]
+    peers = len(packed)
     width = peers * LANES
-    steps = 4 if peers % 4 == 0 else 1
-    spread = pl.BlockSpec((tokens, width // steps), lambda i: (0, i))
     return pl.pallas_call(
-        unpack_kernel,
-        grid=(steps,),
-        in_specs=[pl.BlockSpec((peers // steps, packed.shape[1], LANES), lambda i: (i, 0, 0))],
-        out_specs=[spread] * OUT_ARRAYS
-        + [pl.BlockSpec(short_shape[:2] + (width // steps,), lambda i: (0, 0, i))],
+        functools.partial(unpack_kernel, peers),
+        in_specs=[pl.BlockSpec(memory_space=pltpu.VMEM)] * peers,
+        out_specs=[pl.BlockSpec(memory_space=pltpu.VMEM)] * (OUT_ARRAYS + 1),
         out_shape=[jax.ShapeDtypeStruct((tokens, width), BF16)] * 4
         + [
             jax.ShapeDtypeStruct((tokens, width), F32),
             jax.ShapeDtypeStruct(short_shape, F32),
         ],
         name="unpack_outputs",
-    )(packed)
+    )(*packed)
 
 
 @functools.lru_cache(maxsize=None)
@@ -158,25 +169,18 @@
     return moved
 
 
-def channel_kernel(
-    tokens,
-    grad_scale,
-    packed,
-    weights,
-    forward,
-    backward,
-    out,
-    signals,
-    spectra,
-    high,
-    low,
-    shorts,
-):
-    peers = packed.shape[0]
+def channel_kernel(tokens, peers, grad_scale, *refs):
+    arrived = refs[:peers]
+    weights, forward, backward = refs[peers : peers + 3]
+    out = refs[peers + 3 : 2 * peers + 3]
+    packed, results, signals, spectra, high, low, shorts = refs[2 * peers + 3 :]
     taps = weights.shape[1]
     size = peers * tokens // PHASES
     per = tokens // PHASES
-    at_lanes = pl.ds(pl.multiple_of(lax.axis_index("ctx") * LANES, LANES), LANES)
+    me = lax.axis_index("ctx")
+    at_lanes = pl.ds(pl.multiple_of(me * LANES, LANES), LANES)
+    for step, source in zip(partners(peers), arrived):
+        packed[me ^ step] = source[...]
 
     def phase_of(array, r):
         start = array * tokens + r * per
@@ -229,13 +233,13 @@
         )
         conv.append(result[:, :LANES].astype(BF16).astype(F32))
         conv_grad.append(result[:, LANES : 2 * LANES].astype(BF16).astype(F32))
-        out[:, 4 * tokens + r * per : 4 * tokens + (r + 1) * per, :] = (
+        results[:, 4 * tokens + r * per : 4 * tokens + (r + 1) * per, :] = (
             (result[:, 2 * LANES :] * grad_scale).astype(BF16).reshape(peers, per, LANES)
         )
 
     def put(array, r, value):
         start = array * tokens + r * per
-        out[:, start : start + per, :] = value.astype(BF16).reshape(peers, per, LANES)
+        results[:, start : start + per, :] = value.astype(BF16).reshape(peers, per, LANES)
 
     sums = []
     for array in range(3):
@@ -264,28 +268,31 @@
         piece = rest.astype(BF16).astype(F32)
         pieces.append(piece)
         rest = rest - piece
-    space = out.shape[1] - OUT_ARRAYS * tokens
+    space = results.shape[1] - OUT_ARRAYS * tokens
     filled = PIECES * len(sums)
     if space > filled:
         pieces.append(jnp.zeros((space - filled, LANES), F32))
     block = jnp.concatenate(pieces, axis=0).astype(BF16)
-    for peer in range(peers):
-        out[peer, OUT_ARRAYS * tokens :, :] = block
+    for step, target in zip(partners(peers), out):
+        target[: OUT_ARRAYS * tokens] = results[me ^ step, : OUT_ARRAYS * tokens]
+        target[OUT_ARRAYS * tokens :] = block
 
 
 def channel_step(packed, short_weights, tokens):
-    peers = packed.shape[0]
+    peers = len(packed)
     seq_len = peers * tokens
     size = seq_len // PHASES
     forward, backward = dft_tables(seq_len)
     count = PIECES * short_weights.shape[0] * short_weights.shape[1]
     rows = OUT_ARRAYS * tokens + -(-count // TILE) * TILE
     return pl.pallas_call(
-        functools.partial(channel_kernel, tokens, 1.0 / math.sqrt(seq_len)),
-        in_specs=[pl.BlockSpec(memory_space=pltpu.VMEM)] * 4,
-        out_specs=pl.BlockSpec(memory_space=pltpu.VMEM),
-        out_shape=jax.ShapeDtypeStruct((peers, rows, LANES), BF16),
+        functools.partial(channel_kernel, tokens, peers, 1.0 / math.sqrt(seq_len)),
+        in_specs=[pl.BlockSpec(memory_space=pltpu.VMEM)] * (peers + 3),
+        out_specs=[pl.BlockSpec(memory_space=pltpu.VMEM)] * peers,
+        out_shape=[jax.ShapeDtypeStruct((rows, LANES), BF16)] * peers,
         scratch_shapes=[
+            pltpu.VMEM((peers, IN_ARRAYS * tokens, LANES), BF16),
+            pltpu.VMEM((peers, rows, LANES), BF16),
             pltpu.VMEM((PHASES, size, 3 * LANES), BF16),
             pltpu.VMEM((PHASES, 2 * size, 3 * LANES), F32),
             pltpu.VMEM((PHASES, 2 * size, 3 * LANES), BF16),
@@ -294,17 +301,15 @@
         ],
         compiler_params=pltpu.CompilerParams(vmem_limit_bytes=40 * 1024 * 1024),
         name="channel_operator",
-    )(packed, short_weights, jnp.asarray(forward), jnp.asarray(backward))
+    )(*packed, short_weights, jnp.asarray(forward), jnp.asarray(backward))
 
 
 def channel_shards(query_proj, key_proj, value_proj, cotangent, filter_taps, short_weights):
     peers = lax.axis_size("ctx")
     tokens = query_proj.shape[0]
     packed = pack((query_proj, key_proj, value_proj, cotangent, filter_taps), peers)
-    packed = lax.all_to_all(packed, "ctx", split_axis=0, concat_axis=0, tiled=True)
-    result = channel_step(packed, short_weights, tokens)
-    result = lax.all_to_all(result, "ctx", split_axis=0, concat_axis=0, tiled=True)
-    return tuple(unpack(result, tokens, short_weights.shape))
+    result = channel_step(exchange(packed), short_weights, tokens)
+    return tuple(unpack(exchange(result), tokens, short_weights.shape))
 
 
 def from_behind(array, axis, by):
@@ -500,6 +505,7 @@
     tokens, width = query_proj.shape
     return (
         width == peers * LANES
+        and peers.bit_count() == 1
         and tokens % (PHASES * TILE) == 0
         and peers * tokens <= 2048
     )

time: 59.6 us -> 56.9 us (0.955)
  blocking collectives: 45.5 us -> 0 us
  waiting for transfers between devices: 0 us -> 22.1 us
  starting transfers between devices: 0 us -> 16.3 us
  local copies, waits for them, and re-layouts: 0.01 us -> 6.38 us
  Pallas kernels: 13.1 us -> 11.1 us
    all_to_all x2 -> x0, blocking collectives: 45.5 us -> none  [the longest x1 23.5 us: channel_shards(): lax.all_to_all(packed, 'ctx', split_axis=0, concat_axis=0, tiled=True)]
    ppermute x0 -> x14, waiting for transfers between devices: none -> 22.1 us  [exchange(): lax.ppermute(block, 'ctx', [(i, i ^ step) for i in range(peers)])]
    ppermute x0 -> x14, starting transfers between devices: none -> 16.3 us  [exchange(): lax.ppermute(block, 'ctx', [(i, i ^ step) for i in range(peers)])]
    unnamed x6 -> x24, local copies, waits for them, and re-layouts: 0.01 us -> 6.38 us
    pallas_call x3, Pallas kernels: 13.1 us -> 11.1 us  [the longest x1 5.21 us: channel_step(): pl.pallas_call(functools.partial(channel_kernel, tokens, peers, 1.0 / mat...]
  transfers between devices with their start and end apart: 0 -> 14, of which waited for: 0 -> 9; matrix products, arithmetic and copies ran while one was open for 0% -> 0% of each run, Pallas kernels for 0% -> 0%
where the time goes in v1:
time: 56.9 us; the launch traced here: 56.6 us
  waiting for transfers between devices  22.1 us (39%)
  starting transfers between devices  16.3 us (29%)
  Pallas kernels  11.1 us (20%)
  local copies, waits for them, and re-layouts  6.38 us (11%)
  between operations  0.71 us (1%)
    ppermute x14, waiting for transfers between devices, exchange(): lax.ppermute(block, 'ctx', [(i, i ^ step) for i in range(peers)])  22.1 us
    ppermute x14, starting transfers between devices, exchange(): lax.ppermute(block, 'ctx', [(i, i ^ step) for i in range(peers)])  16.3 us
    unnamed x24, local copies, waits for them, and re-layouts  6.38 us
    pallas_call x1, Pallas kernels, channel_step(): pl.pallas_call(functools.partial(channel_kernel, tokens, peers, 1.0 / mat...  5.21 us
    pallas_call x1, Pallas kernels, unpack(): pl.pallas_call(functools.partial(unpack_kernel, peers), in_specs=[pl.Bloc...  3.07 us
    pallas_call x1, Pallas kernels, pack(): pl.pallas_call(pack_kernel, in_specs=[pl.BlockSpec(memory_space=pltpu.VME...  2.87 us
  transfers between devices with their start and end apart: 14, of which 9 were waited for; matrix products, arithmetic and copies ran while one was open for 0% of the time, Pallas kernels for 0%

profile of v1, /device:TPU:0, one launch (start us, length us, event | category | flops | bytes accessed | tf_op | source)
XLA Modules:
  0.0 56.6 jit_solution(3450337010966194712)
XLA Ops:
  0.6 2.9 %pack_inputs.1 = (bf16[640,128]{1,0:T(8,128)(2,1)}, bf16[640,128]{1,0:T(8,128)(2,1)}, bf16[640,128]{1,0:T(8,128)(2,1)}, bf16[640,128]{1,0:T(8,128)(2,1)}, bf16[6...) custom-call(bf16[128,1024]{1,0:T(8,128)(2,1)} %query.1, ...), custom_call_target="tpu_custom_call" | custom-call | tf_op jit(solution)/shard_map/pack_inputs/pallas_call | solution.py:47
  3.5 3.3 %collective-permute-start = (bf16[640,128]{1,0:T(8,128)(2,1)}, bf16[640,128]{1,0:T(8,128)(2,1)S(1)}, u32[]{:S(2)}, u32[]{:S(2)}) collective-permute-start(bf16[640,128]{1,0:T(8,128)(2,1)} %get-tuple-element.23), channel_id=1, source_target_pairs={{0,28},{4,24},{8,20},{12,16},{16,12},{20,8},{24,4},{28,0},{1,29},{... | collective-permute-start | bytes 491528 | tf_op jit(solution)/shard_map/ppermute | solution.py:60
  6.8 0.6 %collective-permute-start.1 = (bf16[640,128]{1,0:T(8,128)(2,1)}, bf16[640,128]{1,0:T(8,128)(2,1)S(1)}, u32[]{:S(2)}, u32[]{:S(2)}) collective-permute-start(bf16[640,128]{1,0:T(8,128)(2,1)} %get-tuple-element.24), channel_id=1, source_target_pairs={{0,24},{4,28},{8,16},{12,20},{16,8},{20,12},{24,0},{28,4},{1,25},{... | collective-permute-start | bytes 491528 | tf_op jit(solution)/shard_map/ppermute | solution.py:60
  7.4 1.4 %collective-permute-start.2 = (bf16[640,128]{1,0:T(8,128)(2,1)}, bf16[640,128]{1,0:T(8,128)(2,1)S(1)}, u32[]{:S(2)}, u32[]{:S(2)}) collective-permute-start(bf16[640,128]{1,0:T(8,128)(2,1)} %get-tuple-element.25), channel_id=1, source_target_pairs={{0,20},{4,16},{8,28},{12,24},{16,4},{20,0},{24,12},{28,8},{1,21},{... | collective-permute-start | bytes 491528 | tf_op jit(solution)/shard_map/ppermute | solution.py:60
  8.9 0.3 collective-permute-start.3
  9.1 1.2 %collective-permute-start.4 = (bf16[640,128]{1,0:T(8,128)(2,1)}, bf16[640,128]{1,0:T(8,128)(2,1)S(1)}, u32[]{:S(2)}, u32[]{:S(2)}) collective-permute-start(bf16[640,128]{1,0:T(8,128)(2,1)} %get-tuple-element.27), channel_id=1, source_target_pairs={{0,12},{4,8},{8,4},{12,0},{16,28},{20,24},{24,20},{28,16},{1,13},{... | collective-permute-start | bytes 491528 | tf_op jit(solution)/shard_map/ppermute | solution.py:60
  10.3 1.5 %collective-permute-done.refs_1_ = bf16[640,128]{1,0:T(8,128)(2,1)S(1)} collective-permute-done((bf16[640,128]{1,0:T(8,128)(2,1)}, bf16[640,128]{1,0:T(8,128)(2,1)S(1)}, u32[]{:S(2)}, u32[]{:S(2)}) %collective-permute-start) | collective-permute-done | bytes 163872 | tf_op jit(solution)/shard_map/ppermute | solution.py:60
  11.8 2.3 %collective-permute-start.5 = (bf16[640,128]{1,0:T(8,128)(2,1)}, bf16[640,128]{1,0:T(8,128)(2,1)S(1)}, u32[]{:S(2)}, u32[]{:S(2)}) collective-permute-start(bf16[640,128]{1,0:T(8,128)(2,1)} %get-tuple-element.28), channel_id=1, source_target_pairs={{0,8},{4,12},{8,0},{12,4},{16,24},{20,28},{24,16},{28,20},{1,9},{5... | collective-permute-start | bytes 491528 | tf_op jit(solution)/shard_map/ppermute | solution.py:60
  14.1 1.8 %collective-permute-done.1.refs_2_ = bf16[640,128]{1,0:T(8,128)(2,1)S(1)} collective-permute-done((bf16[640,128]{1,0:T(8,128)(2,1)}, bf16[640,128]{1,0:T(8,128)(2,1)S(1)}, u32[]{:S(2)}, u32[]{:S(2)}) %collective-permute-start.1) | collective-permute-done | bytes 163872 | tf_op jit(solution)/shard_map/ppermute | solution.py:60
  15.9 2.9 %collective-permute-done.2.refs_3_ = bf16[640,128]{1,0:T(8,128)(2,1)S(1)} collective-permute-done((bf16[640,128]{1,0:T(8,128)(2,1)}, bf16[640,128]{1,0:T(8,128)(2,1)S(1)}, u32[]{:S(2)}, u32[]{:S(2)}) %collective-permute-start.2) | collective-permute-done | bytes 163872 | tf_op jit(solution)/shard_map/ppermute | solution.py:60
  18.8 3.5 %collective-permute-done.3.refs_4_ = bf16[640,128]{1,0:T(8,128)(2,1)S(1)} collective-permute-done((bf16[640,128]{1,0:T(8,128)(2,1)}, bf16[640,128]{1,0:T(8,128)(2,1)S(1)}, u32[]{:S(2)}, u32[]{:S(2)}) %collective-permute-start.3) | collective-permute-done | bytes 163872 | tf_op jit(solution)/shard_map/ppermute | solution.py:60
  22.3 0.9 %collective-permute-done.5.refs_6_ = bf16[640,128]{1,0:T(8,128)(2,1)S(1)} collective-permute-done((bf16[640,128]{1,0:T(8,128)(2,1)}, bf16[640,128]{1,0:T(8,128)(2,1)S(1)}, u32[]{:S(2)}, u32[]{:S(2)}) %collective-permute-start.5) | collective-permute-done | bytes 163872 | tf_op jit(solution)/shard_map/ppermute | solution.py:60
  23.2 1.6 %copy-done = bf16[4,2,256,512]{3,2,1,0:T(8,128)(2,1)S(1)} copy-done((bf16[4,2,256,512]{3,2,1,0:T(8,128)(2,1)S(1)}, bf16[4,2,256,512]{3,2,1,0:T(8,128)(2,1)}, u32[]{:S(2)}) %copy-start) | copy-done | bytes 2097176
  24.8 1.6 %copy-done.1 = bf16[4,2,512,256]{3,2,1,0:T(8,128)(2,1)S(1)} copy-done((bf16[4,2,512,256]{3,2,1,0:T(8,128)(2,1)S(1)}, bf16[4,2,512,256]{3,2,1,0:T(8,128)(2,1)}, u32[]{:S(2)}) %copy-start.1) | copy-done | bytes 2097176
  26.4 0.9 %copy-done.3 = bf16[640,128]{1,0:T(8,128)(2,1)S(1)} copy-done((bf16[640,128]{1,0:T(8,128)(2,1)S(1)}, bf16[640,128]{1,0:T(8,128)(2,1)}, u32[]{:S(2)}) %copy-start.3) | copy-done | bytes 163864
  27.3 0.8 %copy-done.4 = f32[3,3,1024]{2,1,0:T(4,128)S(1)} copy-done((f32[3,3,1024]{2,1,0:T(4,128)S(1)}, f32[3,3,1024]{2,1,0:T(4,128)}, u32[]{:S(2)}) %copy-start.4) | copy-done | bytes 36888
  28.1 5.2 %channel_operator.1 = (bf16[672,128]{1,0:T(8,128)(2,1)S(1)}, bf16[672,128]{1,0:T(8,128)(2,1)S(1)}, bf16[672,128]{1,0:T(8,128)(2,1)S(1)}, bf16[672,128]{1,0:T(8,1...) custom-call(bf16[640,128]{1,0:T(8,128)(2,1)S(1)} %copy-done.3, ...), custom_call_target="tpu_custom_call" | custom-call | tf_op jit(solution)/shard_map/channel_operator/pallas_call | solution.py:288
  33.3 0.7 %copy-done.2 = bf16[672,128]{1,0:T(8,128)(2,1)} copy-done((bf16[672,128]{1,0:T(8,128)(2,1)}, bf16[672,128]{1,0:T(8,128)(2,1)S(1)}, u32[]{:S(2)}) %copy-start.2) | copy-done | bytes 172056
  34.0 2.0 %collective-permute-start.7 = (bf16[672,128]{1,0:T(8,128)(2,1)S(1)}, bf16[672,128]{1,0:T(8,128)(2,1)S(1)}, u32[]{:S(2)}, u32[]{:S(2)}) collective-permute-start(bf16[672,128]{1,0:T(8,128)(2,1)S(1)} %get-tuple-element.31), channel_id=1, source_target_pairs={{0,28},{4,24},{8,20},{12,16},{16,12},{20,8},{24,4},{28,0},{1,29},{... | collective-permute-start | bytes 516104 | tf_op jit(solution)/shard_map/ppermute | solution.py:60
  36.0 0.6 %collective-permute-start.8 = (bf16[672,128]{1,0:T(8,128)(2,1)S(1)}, bf16[672,128]{1,0:T(8,128)(2,1)S(1)}, u32[]{:S(2)}, u32[]{:S(2)}) collective-permute-start(bf16[672,128]{1,0:T(8,128)(2,1)S(1)} %get-tuple-element.32), channel_id=1, source_target_pairs={{0,24},{4,28},{8,16},{12,20},{16,8},{20,12},{24,0},{28,4},{1,25},{... | collective-permute-start | bytes 516104 | tf_op jit(solution)/shard_map/ppermute | solution.py:60
  36.6 1.2 %collective-permute-start.9 = (bf16[672,128]{1,0:T(8,128)(2,1)S(1)}, bf16[672,128]{1,0:T(8,128)(2,1)S(1)}, u32[]{:S(2)}, u32[]{:S(2)}) collective-permute-start(bf16[672,128]{1,0:T(8,128)(2,1)S(1)} %get-tuple-element.33), channel_id=1, source_target_pairs={{0,20},{4,16},{8,28},{12,24},{16,4},{20,0},{24,12},{28,8},{1,21},{... | collective-permute-start | bytes 516104 | tf_op jit(solution)/shard_map/ppermute | solution.py:60
  37.8 0.6 %collective-permute-start.10 = (bf16[672,128]{1,0:T(8,128)(2,1)S(1)}, bf16[672,128]{1,0:T(8,128)(2,1)S(1)}, u32[]{:S(2)}, u32[]{:S(2)}) collective-permute-start(bf16[672,128]{1,0:T(8,128)(2,1)S(1)} %get-tuple-element.34), channel_id=1, source_target_pairs={{0,16},{4,20},{8,24},{12,28},{16,0},{20,4},{24,8},{28,12},{1,17},{... | collective-permute-start | bytes 516104 | tf_op jit(solution)/shard_map/ppermute | solution.py:60
  38.4 1.2 %collective-permute-start.11 = (bf16[672,128]{1,0:T(8,128)(2,1)S(1)}, bf16[672,128]{1,0:T(8,128)(2,1)S(1)}, u32[]{:S(2)}, u32[]{:S(2)}) collective-permute-start(bf16[672,128]{1,0:T(8,128)(2,1)S(1)} %get-tuple-element.35), channel_id=1, source_target_pairs={{0,12},{4,8},{8,4},{12,0},{16,28},{20,24},{24,20},{28,16},{1,13},{... | collective-permute-start | bytes 516104 | tf_op jit(solution)/shard_map/ppermute | solution.py:60
  39.6 1.8 %collective-permute-done.7.refs_1_ = bf16[672,128]{1,0:T(8,128)(2,1)S(1)} collective-permute-done((bf16[672,128]{1,0:T(8,128)(2,1)S(1)}, bf16[672,128]{1,0:T(8,128)(2,1)S(1)}, u32[]{:S(2)}, u32[]{:S(2)}) %collective-permute-start.7) | collective-permute-done | bytes 172064 | tf_op jit(solution)/shard_map/ppermute | solution.py:60
  41.4 1.5 %collective-permute-start.12 = (bf16[672,128]{1,0:T(8,128)(2,1)S(1)}, bf16[672,128]{1,0:T(8,128)(2,1)S(1)}, u32[]{:S(2)}, u32[]{:S(2)}) collective-permute-start(bf16[672,128]{1,0:T(8,128)(2,1)S(1)} %get-tuple-element.36), channel_id=1, source_target_pairs={{0,8},{4,12},{8,0},{12,4},{16,24},{20,28},{24,16},{28,20},{1,9},{5... | collective-permute-start | bytes 516104 | tf_op jit(solution)/shard_map/ppermute | solution.py:60
  42.9 2.7 %collective-permute-done.8.refs_2_ = bf16[672,128]{1,0:T(8,128)(2,1)S(1)} collective-permute-done((bf16[672,128]{1,0:T(8,128)(2,1)S(1)}, bf16[672,128]{1,0:T(8,128)(2,1)S(1)}, u32[]{:S(2)}, u32[]{:S(2)}) %collective-permute-start.8) | collective-permute-done | bytes 172064 | tf_op jit(solution)/shard_map/ppermute | solution.py:60
  45.6 3.3 %collective-permute-done.9.refs_3_ = bf16[672,128]{1,0:T(8,128)(2,1)S(1)} collective-permute-done((bf16[672,128]{1,0:T(8,128)(2,1)S(1)}, bf16[672,128]{1,0:T(8,128)(2,1)S(1)}, u32[]{:S(2)}, u32[]{:S(2)}) %collective-permute-start.9) | collective-permute-done | bytes 172064 | tf_op jit(solution)/shard_map/ppermute | solution.py:60
  48.9 3.7 %collective-permute-done.10.refs_4_ = bf16[672,128]{1,0:T(8,128)(2,1)S(1)} collective-permute-done((bf16[672,128]{1,0:T(8,128)(2,1)S(1)}, bf16[672,128]{1,0:T(8,128)(2,1)S(1)}, u32[]{:S(2)}, u32[]{:S(2)}) %collective-permute-start.10) | collective-permute-done | bytes 172064 | tf_op jit(solution)/shard_map/ppermute | solution.py:60
  52.7 0.6 %copy-done.8 = bf16[672,128]{1,0:T(8,128)(2,1)} copy-done((bf16[672,128]{1,0:T(8,128)(2,1)}, bf16[672,128]{1,0:T(8,128)(2,1)S(1)}, u32[]{:S(2)}) %copy-start.8) | copy-done | bytes 172056
  53.3 0.1 copy-done.9
  53.4 0.1 copy-done.11
  53.5 3.1 %unpack_outputs.1 = (bf16[128,1024]{1,0:T(8,128)(2,1)}, bf16[128,1024]{1,0:T(8,128)(2,1)}, bf16[128,1024]{1,0:T(8,128)(2,1)}, bf16[128,1024]{1,0:T(8,128)(2,1)},...) custom-call(bf16[672,128]{1,0:T(8,128)(2,1)} %copy-done.2, bf16[672,128]{1,0:T(8,128)(2,1)} %copy-done.5, ...), custom_call_target="tpu_custom_call" | custom-call | tf_op jit(solution)/shard_map/unpack_outputs/pallas_call | solution.py:90
  (23 shorter events, 0.1 us)
Async XLA Ops:
  3.5 8.3 %collective-permute-start = (bf16[640,128]{1,0:T(8,128)(2,1)}, bf16[640,128]{1,0:T(8,128)(2,1)S(1)}, u32[]{:S(2)}, u32[]{:S(2)}) collective-permute-start(bf16[640,128]{1,0:T(8,128)(2,1)} %get-tuple-element.23), channel_id=1, source_target_pairs={{0,28},{4,24},{8,20},{12,16},{16,12},{20,8},{24,4},{28,0},{1,29},{... | collective-permute-start | bytes 491528 | tf_op jit(solution)/shard_map/ppermute | solution.py:60
  6.8 9.0 %collective-permute-start.1 = (bf16[640,128]{1,0:T(8,128)(2,1)}, bf16[640,128]{1,0:T(8,128)(2,1)S(1)}, u32[]{:S(2)}, u32[]{:S(2)}) collective-permute-start(bf16[640,128]{1,0:T(8,128)(2,1)} %get-tuple-element.24), channel_id=1, source_target_pairs={{0,24},{4,28},{8,16},{12,20},{16,8},{20,12},{24,0},{28,4},{1,25},{... | collective-permute-start | bytes 491528 | tf_op jit(solution)/shard_map/ppermute | solution.py:60
  7.4 11.4 %collective-permute-start.2 = (bf16[640,128]{1,0:T(8,128)(2,1)}, bf16[640,128]{1,0:T(8,128)(2,1)S(1)}, u32[]{:S(2)}, u32[]{:S(2)}) collective-permute-start(bf16[640,128]{1,0:T(8,128)(2,1)} %get-tuple-element.25), channel_id=1, source_target_pairs={{0,20},{4,16},{8,28},{12,24},{16,4},{20,0},{24,12},{28,8},{1,21},{... | collective-permute-start | bytes 491528 | tf_op jit(solution)/shard_map/ppermute | solution.py:60
  8.9 13.5 %collective-permute-start.3 = (bf16[640,128]{1,0:T(8,128)(2,1)}, bf16[640,128]{1,0:T(8,128)(2,1)S(1)}, u32[]{:S(2)}, u32[]{:S(2)}) collective-permute-start(bf16[640,128]{1,0:T(8,128)(2,1)} %get-tuple-element.26), channel_id=1, source_target_pairs={{0,16},{4,20},{8,24},{12,28},{16,0},{20,4},{24,8},{28,12},{1,17},{... | collective-permute-start | bytes 491528 | tf_op jit(solution)/shard_map/ppermute | solution.py:60
  9.1 13.2 %collective-permute-start.4 = (bf16[640,128]{1,0:T(8,128)(2,1)}, bf16[640,128]{1,0:T(8,128)(2,1)S(1)}, u32[]{:S(2)}, u32[]{:S(2)}) collective-permute-start(bf16[640,128]{1,0:T(8,128)(2,1)} %get-tuple-element.27), channel_id=1, source_target_pairs={{0,12},{4,8},{8,4},{12,0},{16,28},{20,24},{24,20},{28,16},{1,13},{... | collective-permute-start | bytes 491528 | tf_op jit(solution)/shard_map/ppermute | solution.py:60
  11.8 11.4 %collective-permute-start.5 = (bf16[640,128]{1,0:T(8,128)(2,1)}, bf16[640,128]{1,0:T(8,128)(2,1)S(1)}, u32[]{:S(2)}, u32[]{:S(2)}) collective-permute-start(bf16[640,128]{1,0:T(8,128)(2,1)} %get-tuple-element.28), channel_id=1, source_target_pairs={{0,8},{4,12},{8,0},{12,4},{16,24},{20,28},{24,16},{28,20},{1,9},{5... | collective-permute-start | bytes 491528 | tf_op jit(solution)/shard_map/ppermute | solution.py:60
  15.9 7.3 %collective-permute-start.6 = (bf16[640,128]{1,0:T(8,128)(2,1)}, bf16[640,128]{1,0:T(8,128)(2,1)S(1)}, u32[]{:S(2)}, u32[]{:S(2)}) collective-permute-start(bf16[640,128]{1,0:T(8,128)(2,1)} %get-tuple-element.29), channel_id=1, source_target_pairs={{0,4},{4,0},{8,12},{12,8},{16,20},{20,16},{24,28},{28,24},{1,5},{5... | collective-permute-start | bytes 491528 | tf_op jit(solution)/shard_map/ppermute | solution.py:60
  23.2 1.6 %copy-start = (bf16[4,2,256,512]{3,2,1,0:T(8,128)(2,1)S(1)}, bf16[4,2,256,512]{3,2,1,0:T(8,128)(2,1)}, u32[]{:S(2)}) copy-start(bf16[4,2,256,512]{3,2,1,0:T(8,128)(2,1)} %constant.5.clone.refs_10_) | copy-start | bytes 6291460
  24.8 1.6 %copy-start.1 = (bf16[4,2,512,256]{3,2,1,0:T(8,128)(2,1)S(1)}, bf16[4,2,512,256]{3,2,1,0:T(8,128)(2,1)}, u32[]{:S(2)}) copy-start(bf16[4,2,512,256]{3,2,1,0:T(8,128)(2,1)} %constant.4.clone.refs_9_) | copy-start | bytes 6291460
  26.4 0.9 %copy-start.3 = (bf16[640,128]{1,0:T(8,128)(2,1)S(1)}, bf16[640,128]{1,0:T(8,128)(2,1)}, u32[]{:S(2)}) copy-start(bf16[640,128]{1,0:T(8,128)(2,1)} %get-tuple-element.22.refs_0_) | copy-start | bytes 491524
  27.3 0.8 %copy-start.4 = (f32[3,3,1024]{2,1,0:T(4,128)S(1)}, f32[3,3,1024]{2,1,0:T(4,128)}, u32[]{:S(2)}) copy-start(f32[3,3,1024]{2,1,0:T(4,128)} %refs_8_.1) | copy-start | bytes 110596
  33.3 0.7 %copy-start.2 = (bf16[672,128]{1,0:T(8,128)(2,1)}, bf16[672,128]{1,0:T(8,128)(2,1)S(1)}, u32[]{:S(2)}) copy-start(bf16[672,128]{1,0:T(8,128)(2,1)S(1)} %get-tuple-element.30.refs_0_) | copy-start | bytes 516100
  34.0 7.4 %collective-permute-start.7 = (bf16[672,128]{1,0:T(8,128)(2,1)S(1)}, bf16[672,128]{1,0:T(8,128)(2,1)S(1)}, u32[]{:S(2)}, u32[]{:S(2)}) collective-permute-start(bf16[672,128]{1,0:T(8,128)(2,1)S(1)} %get-tuple-element.31), channel_id=1, source_target_pairs={{0,28},{4,24},{8,20},{12,16},{16,12},{20,8},{24,4},{28,0},{1,29},{... | collective-permute-start | bytes 516104 | tf_op jit(solution)/shard_map/ppermute | solution.py:60
  36.0 9.5 %collective-permute-start.8 = (bf16[672,128]{1,0:T(8,128)(2,1)S(1)}, bf16[672,128]{1,0:T(8,128)(2,1)S(1)}, u32[]{:S(2)}, u32[]{:S(2)}) collective-permute-start(bf16[672,128]{1,0:T(8,128)(2,1)S(1)} %get-tuple-element.32), channel_id=1, source_target_pairs={{0,24},{4,28},{8,16},{12,20},{16,8},{20,12},{24,0},{28,4},{1,25},{... | collective-permute-start | bytes 516104 | tf_op jit(solution)/shard_map/ppermute | solution.py:60
  36.6 12.3 %collective-permute-start.9 = (bf16[672,128]{1,0:T(8,128)(2,1)S(1)}, bf16[672,128]{1,0:T(8,128)(2,1)S(1)}, u32[]{:S(2)}, u32[]{:S(2)}) collective-permute-start(bf16[672,128]{1,0:T(8,128)(2,1)S(1)} %get-tuple-element.33), channel_id=1, source_target_pairs={{0,20},{4,16},{8,28},{12,24},{16,4},{20,0},{24,12},{28,8},{1,21},{... | collective-permute-start | bytes 516104 | tf_op jit(solution)/shard_map/ppermute | solution.py:60
  37.8 14.8 %collective-permute-start.10 = (bf16[672,128]{1,0:T(8,128)(2,1)S(1)}, bf16[672,128]{1,0:T(8,128)(2,1)S(1)}, u32[]{:S(2)}, u32[]{:S(2)}) collective-permute-start(bf16[672,128]{1,0:T(8,128)(2,1)S(1)} %get-tuple-element.34), channel_id=1, source_target_pairs={{0,16},{4,20},{8,24},{12,28},{16,0},{20,4},{24,8},{28,12},{1,17},{... | collective-permute-start | bytes 516104 | tf_op jit(solution)/shard_map/ppermute | solution.py:60
  38.4 14.2 %collective-permute-start.11 = (bf16[672,128]{1,0:T(8,128)(2,1)S(1)}, bf16[672,128]{1,0:T(8,128)(2,1)S(1)}, u32[]{:S(2)}, u32[]{:S(2)}) collective-permute-start(bf16[672,128]{1,0:T(8,128)(2,1)S(1)} %get-tuple-element.35), channel_id=1, source_target_pairs={{0,12},{4,8},{8,4},{12,0},{16,28},{20,24},{24,20},{28,16},{1,13},{... | collective-permute-start | bytes 516104 | tf_op jit(solution)/shard_map/ppermute | solution.py:60
  41.4 11.3 %copy-start.5 = (bf16[672,128]{1,0:T(8,128)(2,1)}, bf16[672,128]{1,0:T(8,128)(2,1)S(1)}, u32[]{:S(2)}) copy-start(bf16[672,128]{1,0:T(8,128)(2,1)S(1)} %collective-permute-done.7.refs_1_) | copy-start | bytes 516100
  41.4 11.3 %collective-permute-start.12 = (bf16[672,128]{1,0:T(8,128)(2,1)S(1)}, bf16[672,128]{1,0:T(8,128)(2,1)S(1)}, u32[]{:S(2)}, u32[]{:S(2)}) collective-permute-start(bf16[672,128]{1,0:T(8,128)(2,1)S(1)} %get-tuple-element.36), channel_id=1, source_target_pairs={{0,8},{4,12},{8,0},{12,4},{16,24},{20,28},{24,16},{28,20},{1,9},{5... | collective-permute-start | bytes 516104 | tf_op jit(solution)/shard_map/ppermute | solution.py:60
  45.6 7.1 %copy-start.6 = (bf16[672,128]{1,0:T(8,128)(2,1)}, bf16[672,128]{1,0:T(8,128)(2,1)S(1)}, u32[]{:S(2)}) copy-start(bf16[672,128]{1,0:T(8,128)(2,1)S(1)} %collective-permute-done.8.refs_2_) | copy-start | bytes 516100
  45.6 7.1 %collective-permute-start.13 = (bf16[672,128]{1,0:T(8,128)(2,1)S(1)}, bf16[672,128]{1,0:T(8,128)(2,1)S(1)}, u32[]{:S(2)}, u32[]{:S(2)}) collective-permute-start(bf16[672,128]{1,0:T(8,128)(2,1)S(1)} %get-tuple-element.37), channel_id=1, source_target_pairs={{0,4},{4,0},{8,12},{12,8},{16,20},{20,16},{24,28},{28,24},{1,5},{5... | collective-permute-start | bytes 516104 | tf_op jit(solution)/shard_map/ppermute | solution.py:60
  48.9 3.8 %copy-start.7 = (bf16[672,128]{1,0:T(8,128)(2,1)}, bf16[672,128]{1,0:T(8,128)(2,1)S(1)}, u32[]{:S(2)}) copy-start(bf16[672,128]{1,0:T(8,128)(2,1)S(1)} %collective-permute-done.9.refs_3_) | copy-start | bytes 516100
  52.6 0.7 %copy-start.8 = (bf16[672,128]{1,0:T(8,128)(2,1)}, bf16[672,128]{1,0:T(8,128)(2,1)S(1)}, u32[]{:S(2)}) copy-start(bf16[672,128]{1,0:T(8,128)(2,1)S(1)} %collective-permute-done.10.refs_4_) | copy-start | bytes 516100
  52.6 0.8 %copy-start.9 = (bf16[672,128]{1,0:T(8,128)(2,1)}, bf16[672,128]{1,0:T(8,128)(2,1)S(1)}, u32[]{:S(2)}) copy-start(bf16[672,128]{1,0:T(8,128)(2,1)S(1)} %collective-permute-done.11.refs_5_) | copy-start | bytes 516100
  52.6 0.8 %copy-start.10 = (bf16[672,128]{1,0:T(8,128)(2,1)}, bf16[672,128]{1,0:T(8,128)(2,1)S(1)}, u32[]{:S(2)}) copy-start(bf16[672,128]{1,0:T(8,128)(2,1)S(1)} %collective-permute-done.12.refs_6_) | copy-start | bytes 516100
  52.6 0.9 %copy-start.11 = (bf16[672,128]{1,0:T(8,128)(2,1)}, bf16[672,128]{1,0:T(8,128)(2,1)S(1)}, u32[]{:S(2)}) copy-start(bf16[672,128]{1,0:T(8,128)(2,1)S(1)} %collective-permute-done.13.refs_7_) | copy-start | bytes 516100
